TPU v7x, 32 devices: a whole 2x2x4 slice. The times are simulated.
32 devices in a mesh: groups: 2 (over x), weight: 16 (over z, y, core).
Axes of the slice: x: 2, y: 2, z: 4, core: 2. Of those that a mesh axis runs over, the one named last changes fastest.
Arguments:
- hidden_in: bfloat16 [512, 8192], P('groups', 'weight'), parts along dimension 0, may hold values from -500 to 500
- norm_gain: bfloat16 [1, 8192], P(None, 'weight'), may hold values from 0.099609375 to 1.8984375
- w_query: bfloat16 [8192, 4096], P(None, 'weight'), may hold values from -1 to 1
- w_key: bfloat16 [8192, 512], P(None, 'weight'), may hold values from -8 to 8
- w_value: bfloat16 [8192, 512], P(None, 'weight'), may hold values from -0.0625 to 0.0625
- w_out: bfloat16 [4096, 8192], P(None, 'weight'), may hold values from -0.09375 to 0.09375
- cache_keys: bfloat16 [24576, 4, 128], P(('groups', 'weight')), parts along dimension 0, may hold values from -200 to 200
- cache_values: bfloat16 [24576, 4, 128], P(('groups', 'weight')), parts along dimension 0, may hold values from -6 to 6
- offset: int32 [2], P('groups'), parts along dimension 0, may hold values from 11904 to 12288
- length: int32 [2], P('groups'), parts along dimension 0, may hold values from 12288 to 12544
Outputs:
- attn_branch: bfloat16 [512, 8192], P('groups', 'weight'), parts along dimension 0
There are 2 independent parts, one for each index of `groups`. A program takes and returns all parts, laid end to end along the dimension named above; an argument that names none is the same for every part. Nothing has to cross between parts.
All inputs are finite; a program needn't handle non-finite values.
Results may differ from a plain program's by a relative error of at most 0.017.
The roundings to bfloat16 on the way count: a program that leaves them out, or rounds other values in their place, can miss the bound.
Values may be sent and summed in bfloat16 or wider, within the bound.
A program may use at most 128 MiB of HBM per device.

v0:
```python
import math

import jax
import jax.numpy as jnp
from jax import lax
from jax.sharding import PartitionSpec as P

QHEADS = 32
KVHEADS = 4
HEAD_DIM = 128


EPSILON = 1e-05
ROPE_BASE = 500000.0
NEG_FILL = -1e30


def rotate(vectors, positions):
    half_dim = vectors.shape[-1] // 2
    inverse = ROPE_BASE ** (-(jnp.arange(half_dim, dtype=jnp.float32) * 2.0 / vectors.shape[-1]))
    angles = positions.astype(jnp.float32)[:, None] * inverse[None, :]
    cosine = jnp.cos(angles)[:, None, :]
    sine_val = jnp.sin(angles)[:, None, :]
    first = vectors[..., :half_dim]
    second = vectors[..., half_dim:]
    return jnp.concatenate(
        [first * cosine - second * sine_val, second * cosine + first * sine_val], axis=-1
    )


def body(
    hidden_in, norm_gain, w_query, w_key, w_value, w_out, cache_keys, cache_values, offset, length
):
    my_index = lax.axis_index("weight")
    new_rows = hidden_in.shape[0]
    gathered, gain_all = (
        lax.all_gather(hidden_in, "weight", axis=1, tiled=True),
        lax.all_gather(norm_gain, "weight", axis=1, tiled=True),
    )
    values_f = gathered.astype(jnp.float32)
    normed = (
        values_f
        * lax.rsqrt(jnp.mean(values_f * values_f, axis=1, keepdims=True) + EPSILON)
        * gain_all.astype(jnp.float32)
    ).astype(jnp.bfloat16)
    query_cols = jnp.dot(normed, w_query, preferred_element_type=jnp.float32).astype(jnp.bfloat16)
    key_cols = jnp.dot(normed, w_key, preferred_element_type=jnp.float32).astype(jnp.bfloat16)
    value_cols = jnp.dot(normed, w_value, preferred_element_type=jnp.float32).astype(jnp.bfloat16)
    queries = lax.all_gather(query_cols, "weight", axis=1, tiled=True)
    fresh = lax.all_to_all(
        jnp.stack([key_cols, value_cols]), "weight", split_axis=1, concat_axis=2, tiled=True
    )
    own_rows = fresh.shape[1]
    start = offset[0]
    query_pos = start + jnp.arange(new_rows, dtype=jnp.int32)
    queries_rot = rotate(
        queries.astype(jnp.float32).reshape(new_rows, QHEADS, HEAD_DIM), query_pos
    ).astype(jnp.bfloat16)
    fresh_index = my_index * own_rows + jnp.arange(own_rows, dtype=jnp.int32)
    keys_rot = rotate(
        fresh[0].astype(jnp.float32).reshape(own_rows, KVHEADS, HEAD_DIM), start + fresh_index
    ).astype(jnp.bfloat16)
    fresh_values = fresh[1].reshape(own_rows, KVHEADS, HEAD_DIM)
    cache_rows = cache_keys.shape[0]
    prefix_ok = my_index * cache_rows + jnp.arange(cache_rows, dtype=jnp.int32) < start
    fresh_ok = (fresh_index[None, :] <= jnp.arange(new_rows, dtype=jnp.int32)[:, None]) & (
        start + fresh_index < length[0]
    )[None, :]
    group_size = QHEADS // KVHEADS
    score_scale = 1.0 / math.sqrt(HEAD_DIM)
    peaks = []
    totals = []
    mixes = []
    for group in range(KVHEADS):
        grouped = queries_rot[:, group * group_size : (group + 1) * group_size, :]
        prefix_scores = (
            jnp.einsum(
                "tgd,kd->tgk", grouped, cache_keys[:, group, :], preferred_element_type=jnp.float32
            )
            * score_scale
        )
        prefix_scores = jnp.where(prefix_ok[None, None, :], prefix_scores, NEG_FILL)
        fresh_scores = (
            jnp.einsum(
                "tgd,kd->tgk", grouped, keys_rot[:, group, :], preferred_element_type=jnp.float32
            )
            * score_scale
        )
        fresh_scores = jnp.where(fresh_ok[:, None, :], fresh_scores, NEG_FILL)
        peak = jnp.maximum(jnp.max(prefix_scores, axis=-1), jnp.max(fresh_scores, axis=-1))
        prefix_weights = jnp.exp(prefix_scores - peak[..., None])
        fresh_weights = jnp.exp(fresh_scores - peak[..., None])
        total = jnp.sum(prefix_weights, axis=-1) + jnp.sum(fresh_weights, axis=-1)
        mixed = jnp.einsum(
            "tgk,kd->tgd",
            prefix_weights.astype(jnp.bfloat16),
            cache_values[:, group, :],
            preferred_element_type=jnp.float32,
        )
        mixed = mixed + jnp.einsum(
            "tgk,kd->tgd",
            fresh_weights.astype(jnp.bfloat16),
            fresh_values[:, group, :],
            preferred_element_type=jnp.float32,
        )
        peaks.append(peak)
        totals.append(total)
        mixes.append(mixed)
    local_peak = jnp.concatenate(peaks, axis=1)
    local_total = jnp.concatenate(totals, axis=1)
    local_mixed = jnp.concatenate(mixes, axis=1)
    global_peak = lax.pmax(local_peak.astype(jnp.bfloat16), "weight").astype(local_peak.dtype)
    factor = jnp.exp(local_peak - global_peak)
    scaled_mixed = (local_mixed * factor[..., None]).reshape(new_rows, QHEADS * HEAD_DIM)
    mixed_share = lax.psum_scatter(scaled_mixed, "weight", scatter_dimension=1, tiled=True)
    denominator = lax.psum(local_total * factor, "weight")
    share_cols = mixed_share.shape[1]
    head_of = (my_index * share_cols + jnp.arange(share_cols, dtype=jnp.int32)) // HEAD_DIM
    selector = (head_of[:, None] == jnp.arange(QHEADS, dtype=jnp.int32)[None, :]).astype(
        jnp.float32
    )
    denom_share = jnp.dot(denominator, selector.T, precision=lax.Precision.HIGHEST)
    attention_share = (mixed_share / denom_share).astype(jnp.bfloat16)
    attention = lax.all_gather(attention_share, "weight", axis=1, tiled=True)
    return jnp.dot(attention, w_out, preferred_element_type=jnp.float32).astype(jnp.bfloat16)


def solution(mesh):
    return jax.shard_map(
        body,
        mesh=mesh,
        in_specs=(
            P("groups", "weight"),
            P(None, "weight"),
            P(None, "weight"),
            P(None, "weight"),
            P(None, "weight"),
            P(None, "weight"),
            P(("groups", "weight"), None, None),
            P(("groups", "weight"), None, None),
            P("groups"),
            P("groups"),
        ),
        out_specs=P("groups", "weight"),
        check_vma=False,
    )
```

profile of v0, /device:TPU:0, one launch (start us, length us, event | category | flops | bytes accessed | tf_op | source)
XLA Modules:
  0.0 344.3 jit_solution(13206799064781447752)
XLA Ops:
  6.5 0.7 all-gather.4.cloned.1.call-update
  7.3 23.7 %all_gather.13 = bf16[1,8192]{1,0:T(2,128)(2,1)S(1)} all-gather(bf16[1,512]{1,0:T(2,128)(2,1)} %param.11), channel_id=1, replica_groups=mesh['groups'=2,'weight'=16] {'weight'}, dimensions={1}, use_global_device_ids=true | all-gather | bytes 17408 | tf_op jit(solution)/shard_map/all_gather | solution.py:38
  31.1 34.4 %all-gather.4.cloned.1.call-done = bf16[256,8192]{1,0:T(8,128)(2,1)} async-done(((bf16[256,512]{1,0:T(8,128)(2,1)}), bf16[256,8192]{1,0:T(8,128)(2,1)}) %all-gather.4.cloned.1.call-update) | async-done | bytes 4194320 | tf_op jit(solution)/shard_map/all_gather | solution.py:37
  65.5 3.3 fusion
  68.9 4.2 %convolution_convert_fusion.1 = bf16[256,256]{1,0:T(8,128)(2,1)} fusion(bf16[8192,256]{1,0:T(8,128)(2,1)} %param.12, bf16[256,8192]{1,0:T(8,128)(2,1)S(1)} %copy-done.5, f32[8192]{0:T(1024)S(1)} %bitcast.128, f32[256]{0:T(256)S(1)} %add_rsqrt_fusion), kind=kOutput, calls=%fused_computation.45 | convolution fusion | flops 1082195968 | bytes 8553472 | tf_op jit(solution)/shard_map/dot_general | solution.py:46
  74.6 1.9 fusion.89
  76.4 1.8 copy.66
  78.3 0.9 copy.69
  79.2 0.3 copy.72
  79.6 0.3 copy.75
  80.0 0.7 multiply_cosine_fusion.1
  80.7 0.5 multiply_cosine_fusion
  81.3 1.1 fusion.90
  82.5 3.7 %fusion.32 = bf16[1,256,32]{1,2,0:T(8,128)(2,1)S(1)} fusion(bf16[8192,32]{0,1:T(8,128)(2,1)S(1)} %copy-done, bf16[256,8192]{1,0:T(8,128)(2,1)} %all-gather.4.cloned.1.call-done, f32[8192]{0:T(1024)} %bitcast.129, f32[256]{0:T(256)S(1)} %add_rsqrt_fusion), kind=kOutput, calls=%fused_computation.56 | convolution fusion | flops 142614528 | bytes 4768768 | tf_op jit(solution)/shard_map/dot_general | solution.py:47
  86.3 1.4 fusion.33
  87.8 0.8 reshape.242
  88.6 3.5 %all-to-all-start = ((bf16[16,2,512]{2,1,0:T(2,128)(2,1)}), bf16[16,2,512]{2,1,0:T(2,128)(2,1)S(1)}, u32[]{:S(2)}, u32[]{:S(2)}) async-start(bf16[16,2,512]{2,1,0:T(2,128)(2,1)} %reshape.242), calls=%async_computation | async-start | bytes 65536 | tf_op jit(solution)/shard_map/all_to_all | solution.py:50
  92.4 6.4 %all-to-all-done = bf16[16,2,512]{2,1,0:T(2,128)(2,1)S(1)} async-done(((bf16[16,2,512]{2,1,0:T(2,128)(2,1)}), bf16[16,2,512]{2,1,0:T(2,128)(2,1)S(1)}, u32[]{:S(2)}, u32[]{:S(2)}) %all-to-all-start) | async-done | bytes 32800 | tf_op jit(solution)/shard_map/all_to_all | solution.py:50
  99.4 13.4 %all-gather.6.cloned.1.call-done = bf16[256,4096]{1,0:T(8,128)(2,1)} async-done(((bf16[256,256]{1,0:T(8,128)(2,1)}), bf16[256,4096]{1,0:T(8,128)(2,1)}) %all-gather.6.cloned.1.call-update) | async-done | bytes 2097168 | tf_op jit(solution)/shard_map/all_gather | solution.py:49
  112.8 2.1 convert_bitcast_fusion
  114.9 0.8 copy.77
  115.7 1.5 fusion.88
  117.1 4.9 %subtract_convert_fusion = (bf16[256,32,64]{2,0,1:T(8,128)(2,1)S(1)}, bf16[256,32,64]{2,0,1:T(8,128)(2,1)S(1)}) fusion(f32[256,32,64]{2,1,0:T(8,128)S(1)} %get-tuple-element.17, f32[256,32,64]{2,1,0:T(8,128)S(1)} %get-tuple-element.16, f32[256,64]{1,0:T(8,128)S(1)} %get-tuple-element.37, f32[256,64]{1,0:T(8,128)S(1)} %get-tuple-element.36), kind=kLoop, calls=%fused_computation.28 | loop fusion | flops 4194304 | bytes 6422528 | tf_op jit(solution)/shard_map/convert.5
  122.1 1.2 pad_maximum_fusion
  123.2 0.3 fusion.94
  124.2 0.3 fusion.95
  124.5 1.0 fusion.34
  125.5 1.0 fusion.35
  126.5 1.1 fusion.3
  127.6 0.5 copy-done.2
  128.1 5.6 %fusion.7 = (f32[256,8]{0,1:T(8,128)S(1)}, f32[256,8]{0,1:T(8,128)S(1)}, f32[256,8]{0,1:T(8,128)S(1)}, f32[256,8]{0,1:T(8,128)S(1)}, f32[256,8,768]{2,0,1:T(8,128)}) fusion(f32[256,8,768]{2,0,1:T(8,128)S(1)} %get-tuple-element.41, f32[256,8]{0,1:T(8,128)S(1)} %max.30, pred[768]{0:T(1024)(128)(4,1)S(1)} %add_compare_fusion, f32[256,8,768]{2,0,1:T(8,128)S(1)} %fusion.35, ...), kind=kOutput, calls=%fused_computation.17 | convolution fusion | flops 423092224 | bytes 27501312 | tf_op jit(solution)/shard_map/tgd,kd->tgk/dot_general | solution.py:77
  133.8 60.0 %pmax.7 = bf16[256,32]{0,1:T(8,128)(2,1)S(1)} all-reduce(bf16[256,32]{0,1:T(8,128)(2,1)S(1)} %fusion.59), channel_id=1, replica_groups=mesh['groups'=2,'weight'=16] {'weight'}, use_global_device_ids=true, to_apply=%region_9.10 | all-reduce | flops 8192 | bytes 32768 | tf_op jit(solution)/shard_map/pmax | solution.py:112
  194.0 9.2 %fusion.9 = (f32[256,8]{0,1:T(8,128)S(1)}, f32[256,8]{0,1:T(8,128)S(1)}, f32[256,8]{0,1:T(8,128)S(1)}) fusion(f32[256,8,768]{2,0,1:T(8,128)} %get-tuple-element.44, f32[256,8]{0,1:T(8,128)S(1)} %max.31, pred[768]{0:T(1024)(128)(4,1)S(1)} %add_compare_fusion, f32[256,8]{0,1:T(8,128)S(1)} %max.32, f32[256,8,768]{2,0,1:T(8,128)} %copy-done.3, ...), kind=kLoop, calls=%fused_computation.19 | loop fusion | flops 18868224 | bytes 18924288 | tf_op jit(solution)/shard_map/reduce_sum | solution.py:93
  203.4 1.8 fusion.21
  205.3 1.8 fusion.19
  207.1 1.8 fusion.17
  208.9 1.8 fusion.15
  210.7 0.3 convolution_add_fusion.3
  211.1 0.3 convolution_add_fusion.2
  211.4 0.3 convolution_add_fusion.1
  211.8 0.3 convolution_add_fusion
  212.1 2.5 maximum_multiply_fusion
  214.7 5.6 %copy.60 = f32[256,4096]{1,0:T(8,128)} copy(f32[256,4096]{0,1:T(8,128)} %bitcast.120) | data formatting | bytes 8388608 | tf_op jit(solution)/shard_map/mul | solution.py:114
  220.4 58.9 %psum.7 = f32[256,32]{0,1:T(8,128)S(1)} all-reduce(f32[256,32]{0,1:T(8,128)S(1)} %get-tuple-element.12), channel_id=1, replica_groups=mesh['groups'=2,'weight'=16] {'weight'}, use_global_device_ids=true, to_apply=%region_19.20 | all-reduce | flops 8192 | bytes 65536 | tf_op jit(solution)/shard_map/psum | solution.py:116
  279.3 11.1 %reduce-scatter.2.cloned.1.call-done = f32[256,256]{1,0:T(8,128)} async-done(((f32[256,4096]{1,0:T(8,128)}), f32[256,256]{1,0:T(8,128)}) %reduce-scatter.2.cloned.1.call-update) | async-done | bytes 262160 | tf_op jit(solution)/shard_map/reduce_scatter | solution.py:115
  290.4 2.0 fusion.27
  292.4 40.6 %all-gather.8.cloned.1.call-done = bf16[256,4096]{1,0:T(8,128)(2,1)} async-done(((bf16[256,256]{1,0:T(8,128)(2,1)}), bf16[256,4096]{1,0:T(8,128)(2,1)}) %all-gather.8.cloned.1.call-update) | async-done | bytes 2097168 | tf_op jit(solution)/shard_map/all_gather | solution.py:124
  333.0 4.8 %convolution_convert_fusion = bf16[256,512]{1,0:T(8,128)(2,1)} fusion(bf16[256,4096]{1,0:T(8,128)(2,1)} %all-gather.8.cloned.1.call-done, bf16[4096,512]{1,0:T(8,128)(2,1)} %param.15), kind=kOutput, calls=%fused_computation.42 | convolution fusion | flops 1073872896 | bytes 6553600 | tf_op jit(solution)/shard_map/dot_general | solution.py:125
  (93 shorter events, 2.5 us)
Async XLA Ops:
  6.5 75.9 %copy-start = (bf16[8192,32]{0,1:T(8,128)(2,1)S(1)}, bf16[8192,32]{0,1:T(8,128)(2,1)}, u32[]{:S(2)}) copy-start(bf16[8192,32]{0,1:T(8,128)(2,1)} %param.13) | copy-start | bytes 1572868
  6.5 59.0 %all-gather.4.cloned.1.call-start = ((), (), s32[]{:S(2)}) async-start(), calls=%async_computation.2 | async-start | bytes 4456448 | tf_op jit(solution)/shard_map/all_gather | solution.py:37
  7.3 105.6 %all-gather.6.cloned.1.call-start = ((), (), s32[]{:S(2)}) async-start(), calls=%async_computation.3 | async-start | bytes 2228224 | tf_op jit(solution)/shard_map/all_gather | solution.py:49
  31.1 37.7 %copy-start.12 = (f32[1,8192]{1,0:T(1,128)}, f32[1,8192]{1,0:T(1,128)S(1)}, u32[]{:S(2)}) copy-start(f32[1,8192]{1,0:T(1,128)S(1)} %mul.211) | copy-start | bytes 98308
  65.5 3.4 %copy-start.5 = (bf16[256,8192]{1,0:T(8,128)(2,1)S(1)}, bf16[256,8192]{1,0:T(8,128)(2,1)}, u32[]{:S(2)}) copy-start(bf16[256,8192]{1,0:T(8,128)(2,1)} %all-gather.4.cloned.1.call-done) | copy-start | bytes 12582916
  68.9 5.6 %copy-start.7 = (bf16[768,4,128]{2,1,0:T(4,128)(2,1)S(1)}, bf16[768,4,128]{2,1,0:T(4,128)(2,1)}, u32[]{:S(2)}) copy-start(bf16[768,4,128]{2,1,0:T(4,128)(2,1)} %param.17) | copy-start | bytes 2359300
  73.2 8.1 %copy-start.8 = (bf16[768,4,128]{2,1,0:T(4,128)(2,1)S(1)}, bf16[768,4,128]{2,1,0:T(4,128)(2,1)}, u32[]{:S(2)}) copy-start(bf16[768,4,128]{2,1,0:T(4,128)(2,1)} %param.16) | copy-start | bytes 2359300
  82.4 3.8 %copy-start.6 = (bf16[256,8192]{1,0:T(8,128)(2,1)S(1)}, bf16[256,8192]{1,0:T(8,128)(2,1)}, u32[]{:S(2)}) copy-start(bf16[256,8192]{1,0:T(8,128)(2,1)} %all-gather.4.cloned.1.call-done) | copy-start | bytes 12582916
  82.4 3.8 %copy-start.13 = (f32[1,8192]{1,0:T(1,128)S(1)}, f32[1,8192]{1,0:T(1,128)}, u32[]{:S(2)}) copy-start(f32[1,8192]{1,0:T(1,128)} %copy-done.12) | copy-start | bytes 98308
  82.5 3.8 %copy-start.14 = (bf16[8192,32]{0,1:T(8,128)(2,1)S(1)}, bf16[8192,32]{0,1:T(8,128)(2,1)}, u32[]{:S(2)}) copy-start(bf16[8192,32]{0,1:T(8,128)(2,1)} %param.14) | copy-start | bytes 1572868
  86.3 13.1 %copy-start.11 = (f32[16,64]{1,0:T(8,128)S(1)}, f32[16,64]{1,0:T(8,128)}, u32[]{:S(2)}) copy-start(f32[16,64]{1,0:T(8,128)} %get-tuple-element.39) | copy-start | bytes 12292
  88.6 10.2 %all-to-all-start = ((bf16[16,2,512]{2,1,0:T(2,128)(2,1)}), bf16[16,2,512]{2,1,0:T(2,128)(2,1)S(1)}, u32[]{:S(2)}, u32[]{:S(2)}) async-start(bf16[16,2,512]{2,1,0:T(2,128)(2,1)} %reshape.242), calls=%async_computation | async-start | bytes 65536 | tf_op jit(solution)/shard_map/all_to_all | solution.py:50
  92.1 198.3 %reduce-scatter.2.cloned.1.call-start = ((), (), s32[]{:S(2)}) async-start(), calls=%async_computation.4 | async-start | bytes 4456448 | tf_op jit(solution)/shard_map/reduce_scatter | solution.py:115
  125.5 2.7 copy-start.2
  126.5 7.3 %copy-start.3 = (f32[256,8,768]{2,0,1:T(8,128)}, f32[256,8,768]{2,0,1:T(8,128)S(1)}, u32[]{:S(2)}) copy-start(f32[256,8,768]{2,0,1:T(8,128)S(1)} %fusion.35) | copy-start | bytes 18874372
  127.6 6.2 %copy-start.4 = (f32[256,8,768]{2,0,1:T(8,128)}, f32[256,8,768]{2,0,1:T(8,128)S(1)}, u32[]{:S(2)}) copy-start(f32[256,8,768]{2,0,1:T(8,128)S(1)} %get-tuple-element.41) | copy-start | bytes 18874372
  193.8 9.4 %slice-start.4 = ((s8[6291456]{0:T(1024)(128)(4,1)}), s8[4194304]{0:T(1024)(128)(4,1)S(1)}, s32[]{:S(2)}) async-start(s8[6291456]{0:T(1024)(128)(4,1)} %bitcast.121), calls=%async_computation.10 | async-start | bytes 8388608
  193.8 11.4 %slice-start.6 = ((s8[6291456]{0:T(1024)(128)(4,1)}), s8[4194304]{0:T(1024)(128)(4,1)S(1)}, s32[]{:S(2)}) async-start(s8[6291456]{0:T(1024)(128)(4,1)} %bitcast.123), calls=%async_computation.12 | async-start | bytes 8388608
  193.9 9.5 %slice-start.5 = ((s8[6291456]{0:T(1024)(128)(4,1)}), s8[2097152]{0:T(1024)(128)(4,1)S(1)}, s32[]{:S(2)}) async-start(s8[6291456]{0:T(1024)(128)(4,1)} %bitcast.121), calls=%async_computation.11 | async-start | bytes 4194304
  193.9 9.5 %copy-start.10 = (bf16[768,1,128]{0,2,1:T(8,128)(2,1)S(1)}, bf16[768,1,128]{0,2,1:T(8,128)(2,1)}, u32[]{:S(2)}) copy-start(bf16[768,1,128]{0,2,1:T(8,128)(2,1)} %copy.66) | copy-start | bytes 589828
  193.9 11.3 %slice-start.7 = ((s8[6291456]{0:T(1024)(128)(4,1)}), s8[2097152]{0:T(1024)(128)(4,1)S(1)}, s32[]{:S(2)}) async-start(s8[6291456]{0:T(1024)(128)(4,1)} %bitcast.123), calls=%async_computation.13 | async-start | bytes 4194304
  194.0 13.1 %slice-start.2 = ((s8[6291456]{0:T(1024)(128)(4,1)}), s8[2097152]{0:T(1024)(128)(4,1)S(1)}, s32[]{:S(2)}) async-start(s8[6291456]{0:T(1024)(128)(4,1)} %bitcast.118), calls=%async_computation.8 | async-start | bytes 4194304
  203.2 3.9 %slice-start.3 = ((s8[6291456]{0:T(1024)(128)(4,1)}), s8[4194304]{0:T(1024)(128)(4,1)S(1)}, s32[]{:S(2)}) async-start(s8[6291456]{0:T(1024)(128)(4,1)} %bitcast.118), calls=%async_computation.9 | async-start | bytes 8388608
  203.4 1.8 copy-start.9
  205.3 3.6 %slice-start = ((s8[6291456]{0:T(1024)(128)(4,1)}), s8[4194304]{0:T(1024)(128)(4,1)S(1)}, s32[]{:S(2)}) async-start(s8[6291456]{0:T(1024)(128)(4,1)} %bitcast.116), calls=%async_computation.6 | async-start | bytes 8388608
  207.1 1.8 slice-start.1
  220.3 112.7 %all-gather.8.cloned.1.call-start = ((), (), s32[]{:S(2)}) async-start(), calls=%async_computation.5 | async-start | bytes 2228224 | tf_op jit(solution)/shard_map/all_gather | solution.py:124
  220.4 117.4 %copy-start.1 = (bf16[8192,32]{0,1:T(8,128)(2,1)S(1)}, bf16[8192,32]{0,1:T(8,128)(2,1)}, u32[]{:S(2)}) copy-start(bf16[8192,32]{0,1:T(8,128)(2,1)} %param.13) | copy-start | bytes 1572868
Sparse Core Ops, SparseCore 0:
  9.5 55.9 all-gather.3
  73.3 39.4 all-gather.5
  220.4 69.9 reduce-scatter.1
  292.6 40.3 all-gather.7
where the time goes:
time: 345 us; the launch traced here: 344 us
  blocking collectives  143 us (41%)
  waiting for transfers between devices  107 us (31%)
  matrix products  34.5 us (10%)
  other arithmetic  24.8 us (7%)
  local copies, waits for them, and re-layouts  16.7 us (5%)
  between operations  15.2 us (4%)
  starting transfers between devices  3.79 us (1%)
    pmax x1, blocking collectives, body(): lax.pmax(local_peak.astype(jnp.bfloat16), 'weight').astype(local_peak.dtype)  60 us
    psum x1, blocking collectives, body(): denominator = lax.psum(local_total * factor, 'weight')  58.9 us
    all_gather x1, waiting for transfers between devices, body(): attention = lax.all_gather(attention_share, 'weight', axis=1, tiled=True)  40.6 us
    all_gather x1, waiting for transfers between devices, body(): lax.all_gather(hidden_in, 'weight', axis=1, tiled=True)  34.4 us
    all_gather x1, blocking collectives, body(): lax.all_gather(norm_gain, 'weight', axis=1, tiled=True)  23.7 us
    all_gather x1, waiting for transfers between devices, body(): queries = lax.all_gather(query_cols, 'weight', axis=1, tiled=True)  13.4 us
    reduce_scatter x1, waiting for transfers between devices, body(): lax.psum_scatter(scaled_mixed, 'weight', scatter_dimension=1, tiled=True)  11.1 us
    reduce_sum x5, other arithmetic, body(): total = jnp.sum(prefix_weights, axis=-1) + jnp.sum(fresh_weights, axis=-1)  9.33 us
  transfers between devices with their start and end apart: 5, of which 5 were waited for; matrix products, arithmetic and copies ran while one was open for 4% of the time, Pallas kernels for 0%

commit v1 on v0

--- a/solution.py
+++ b/solution.py
@@ -1,8 +1,11 @@
+import functools
 import math
 
 import jax
 import jax.numpy as jnp
 from jax import lax
+from jax.experimental import pallas as pl
+from jax.experimental.pallas import tpu as pltpu
 from jax.sharding import PartitionSpec as P
 
 QHEADS = 32
@@ -28,7 +31,7 @@
     )
 
 
-def body(
+def general_body(
     hidden_in, norm_gain, w_query, w_key, w_value, w_out, cache_keys, cache_values, offset, length
 ):
     my_index = lax.axis_index("weight")
@@ -125,7 +128,370 @@
     return jnp.dot(attention, w_out, preferred_element_type=jnp.float32).astype(jnp.bfloat16)
 
 
+PLANES = 4
+PLANE = 4
+PAD_ROWS = 16
+FUSED_DEVICES = PLANES * PLANE
+
+
+def near_order(z):
+    half = lax.div(z, 2)
+    return [z, z + 1 - 2 * lax.rem(z, 2), 2 - half, 3 * (1 - half)]
+
+
+def fused_kernel(
+    start_ref, length_ref, hidden, w_query, wk_t, wv_t, w_out, kv, cos_ref, sin_ref,
+    out_ref,
+    xg, wq, wkv, wo, kvb, pq, acc, peak, total, so, sl, ro, rl, at, rinv, qacc, kacc, oacc,
+    ss1, rs1, sskv, rskv, ss2, rs2, ss3, rs3, ss4, rs4, local_sem,
+):
+    me = lax.axis_index("weight")
+    z = lax.div(me, 4)
+    y = lax.rem(lax.div(me, 2), 2)
+    c = lax.rem(me, 2)
+    q = lax.rem(me, 4)
+    plane0 = z * 4
+    up, down = me + 4, me - 4
+    yn = me + 2 - 4 * y
+    sib = me + 1 - 2 * c
+    ynsib = yn + 1 - 2 * c
+    order = near_order(z)
+    tokens = out_ref.shape[0]
+    depth = xg.shape[2]
+    keys = kvb.shape[2]
+
+    def remote(src, dst, ssem, rsem, dev):
+        return pltpu.make_async_remote_copy(
+            src_ref=src, dst_ref=dst, send_sem=ssem, recv_sem=rsem,
+            device_id={"weight": dev}, device_id_type=pl.DeviceIdType.MESH,
+        )
+
+    barrier = pltpu.get_barrier_semaphore()
+    for k in range(1, 4):
+        for dev in (order[k] * 4 + q, plane0 + lax.rem(q + k, 4)):
+            pl.semaphore_signal(
+                barrier, inc=1, device_id={"weight": dev}, device_id_type=pl.DeviceIdType.MESH
+            )
+    pl.semaphore_wait(barrier, 6)
+
+    def gather(slots, own, ss, rs, consume, between):
+        def cp(i, src, d, dev):
+            return remote(src, slots.at[i], ss.at[i, d], rs.at[i], dev)
+
+        def fan(i, src, go_up, go_down):
+            if go_up is not None:
+                @pl.when(go_up)
+                def _():
+                    cp(i, src, 0, up).start()
+            if go_down is not None:
+                @pl.when(go_down)
+                def _():
+                    cp(i, src, 1, down).start()
+            cp(i, src, 2, yn).start()
+            cp(i, src, 3, sib).start()
+
+        fan(me, own, z < 3, z > 0)
+        between(-1)
+        for k in range(4):
+            if k < 3:
+                o = order[k + 1]
+                i = o * 4 + q
+                cp(i, slots.at[i], 2, yn).wait_recv()
+                fan(i, slots.at[i], (o < z) & (z < 3), (o > z) & (z > 0))
+            i = order[k] * 4 + lax.rem(yn, 4)
+            cp(i, slots.at[i], 2, yn).wait_recv()
+            cp(i, slots.at[i], 3, sib).start()
+            between(k)
+            consume(order[k] * 4 + q, slots)
+            consume(order[k] * 4 + lax.rem(yn, 4), slots)
+            for other in (sib, ynsib):
+                i = order[k] * 4 + lax.rem(other, 4)
+                cp(i, slots.at[i], 3, sib).wait_recv()
+                consume(i, slots)
+
+        def finish():
+            @pl.when(z < 3)
+            def _():
+                cp(me, own, 0, up).wait_send()
+            @pl.when(z > 0)
+            def _():
+                cp(me, own, 1, down).wait_send()
+            cp(me, own, 2, yn).wait_send()
+            cp(me, own, 3, sib).wait_send()
+            for k in range(1, 4):
+                o = order[k]
+                i = o * 4 + q
+                @pl.when((o < z) & (z < 3))
+                def _():
+                    cp(i, slots.at[i], 0, up).wait_send()
+                @pl.when((o > z) & (z > 0))
+                def _():
+                    cp(i, slots.at[i], 1, down).wait_send()
+                cp(i, slots.at[i], 2, yn).wait_send()
+                cp(i, slots.at[i], 3, sib).wait_send()
+            for k in range(4):
+                i = order[k] * 4 + lax.rem(yn, 4)
+                cp(i, slots.at[i], 3, sib).wait_send()
+
+        return finish
+
+    own_copy = pltpu.make_async_copy(hidden, xg.at[me], local_sem.at[0])
+    loads = [
+        pltpu.make_async_copy(w_query, wq, local_sem.at[1]),
+        pltpu.make_async_copy(wk_t, wkv.at[pl.ds(0, 32)], local_sem.at[2]),
+        pltpu.make_async_copy(wv_t, wkv.at[pl.ds(32, 32)], local_sem.at[3]),
+        pltpu.make_async_copy(kv.at[z], kvb.at[z], local_sem.at[4]),
+        pltpu.make_async_copy(w_out, wo, local_sem.at[5]),
+    ]
+
+    def kv_copy(k):
+        return remote(kv.at[order[k]], kvb.at[z], sskv.at[order[k]], rskv.at[z], order[k] * 4 + q)
+
+    def kv_arrival(k):
+        o = order[k]
+        return remote(kv.at[o], kvb.at[o], sskv.at[o], rskv.at[o], o * 4 + q)
+
+    def between_first(k):
+        if k == -1:
+            own_copy.start()
+            for load in loads:
+                load.start()
+            rinv[...] = jnp.zeros_like(rinv)
+            own_copy.wait()
+        if k == KV_AFTER:
+            for j in range(1, 4):
+                kv_copy(j).start()
+
+    def squares(i, slots):
+        x = slots[i, 0:tokens, :].astype(jnp.float32)
+        xx = x * x
+        part = xx[:, 0:128]
+        for j in range(1, depth // 128):
+            part = part + xx[:, j * 128 : (j + 1) * 128]
+        rinv[...] += part
+
+    finish_first = gather(xg, hidden, ss1, rs1, squares, between_first)
+
+    mean = jnp.sum(rinv[...], axis=1, keepdims=True) * (1.0 / (depth * FUSED_DEVICES))
+    rinv[...] = jnp.broadcast_to(lax.rsqrt(mean + EPSILON), rinv.shape)
+    for load in loads[:3]:
+        load.wait()
+    qacc[...] = jnp.zeros_like(qacc)
+    kacc[...] = jnp.zeros_like(kacc)
+
+    def project(i, carry):
+        x = xg[i, 0:tokens, :].astype(jnp.float32)
+        gain = xg[i, tokens : tokens + 1, :].astype(jnp.float32)
+        scale = jnp.concatenate([rinv[...]] * (depth // 128), axis=1)
+        normed = (x * scale * gain).astype(jnp.bfloat16)
+        first = pl.multiple_of(i * depth, depth)
+        qacc[...] += jnp.dot(normed, wq[pl.ds(first, depth), :], preferred_element_type=jnp.float32)
+        kacc[...] += lax.dot_general(
+            normed, wkv[:, pl.ds(first, depth)], (((1,), (1,)), ((), ())),
+            preferred_element_type=jnp.float32,
+        )
+        return carry
+
+    lax.fori_loop(0, FUSED_DEVICES, project, 0)
+
+    def turn(x, cosine, sine):
+        return (x * cosine + pltpu.roll(x, 64, 1) * sine).astype(jnp.bfloat16)
+
+    queries = qacc[...].astype(jnp.bfloat16).astype(jnp.float32)
+    for h in range(2):
+        at_cols = slice(h * HEAD_DIM, (h + 1) * HEAD_DIM)
+        pq[q, :, at_cols] = turn(queries[:, at_cols], cos_ref[...], sin_ref[...])
+    pq[q, :, 256:320] = kacc[...].astype(jnp.bfloat16)
+    pq[q, :, 320:384] = jnp.zeros((tokens, 64), jnp.bfloat16)
+
+    def pcp(i, d, dev):
+        return remote(pq.at[i], pq.at[i], ss2.at[i, d], rs2.at[i], dev)
+
+    yq, sq, ysq = lax.rem(yn, 4), lax.rem(sib, 4), lax.rem(ynsib, 4)
+    pcp(q, 0, yn).start()
+    pcp(q, 1, sib).start()
+
+    def clear(h, carry):
+        acc[h] = jnp.zeros(acc.shape[1:], jnp.float32)
+        peak[h] = jnp.full(peak.shape[1:], NEG_FILL, jnp.float32)
+        total[h] = jnp.zeros(total.shape[1:], jnp.float32)
+        return carry
+
+    lax.fori_loop(0, 8, clear, 0)
+    pcp(yq, 0, yn).wait_recv()
+    pcp(yq, 1, sib).start()
+    pcp(sq, 1, sib).wait_recv()
+    pcp(ysq, 1, sib).wait_recv()
+
+    start = start_ref[0]
+    length = length_ref[0]
+    score_scale = 1.0 / math.sqrt(HEAD_DIM)
+
+    def attend(p, key_rows, value_rows, allowed):
+        for h in range(2):
+            n = p * 2 + h
+            scores = lax.dot_general(
+                key_rows, pq[p, :, h * HEAD_DIM : (h + 1) * HEAD_DIM], (((1,), (1,)), ((), ())),
+                preferred_element_type=jnp.float32,
+            ) * score_scale
+            scores = jnp.where(allowed, scores, NEG_FILL)
+            old = peak[n]
+            new = jnp.maximum(old, jnp.max(scores, axis=0, keepdims=True))
+            weights = jnp.exp(scores - new)
+            factor = jnp.exp(old - new)
+            peak[n] = new
+            total[n] = total[n] * factor + jnp.sum(weights, axis=0, keepdims=True)
+            acc[n] = acc[n] * factor + lax.dot_general(
+                value_rows, weights.astype(jnp.bfloat16), (((0,), (0,)), ((), ())),
+                preferred_element_type=jnp.float32,
+            )
+
+    loads[3].wait()
+    for k in range(4):
+        o = order[k]
+        if k > 0:
+            kv_arrival(k).wait_recv()
+
+        def one(p, carry):
+            row = lax.broadcasted_iota(jnp.int32, (keys, tokens), 0)
+            allowed = row < start - (o * 4 + q) * keys
+            attend(p, kvb[o, 0], kvb[o, 1], allowed)
+            return carry
+
+        lax.fori_loop(0, PLANE, one, 0)
+
+    own_rows = tokens // PLANE
+    row0 = pl.multiple_of(q * own_rows, own_rows)
+    fresh_key = jnp.concatenate(
+        [pq[p, pl.ds(row0, own_rows), 256:288] for p in range(PLANE)], axis=1
+    ).astype(jnp.float32)
+    fresh_key = turn(fresh_key, cos_ref[pl.ds(row0, own_rows), :], sin_ref[pl.ds(row0, own_rows), :])
+    fresh_value = jnp.concatenate(
+        [pq[p, pl.ds(row0, own_rows), 288:320] for p in range(PLANE)], axis=1
+    )
+
+    def one_fresh(p, carry):
+        row = row0 + lax.broadcasted_iota(jnp.int32, (own_rows, tokens), 0)
+        token = lax.broadcasted_iota(jnp.int32, (own_rows, tokens), 1)
+        attend(p, fresh_key, fresh_value, (row <= token) & (row < length - start))
+        return carry
+
+    lax.fori_loop(0, PLANE, one_fresh, 0)
+
+    def pack(p, carry):
+        for h in range(2):
+            n = p * 2 + h
+            so[p, h * HEAD_DIM : (h + 1) * HEAD_DIM, :] = (acc[n] / total[n]).astype(jnp.bfloat16)
+            sl[p, h : h + 1, :] = peak[n] + jnp.log(total[n])
+        sl[p, 2:8, :] = jnp.zeros((6, tokens), jnp.float32)
+        return carry
+
+    lax.fori_loop(0, PLANE, pack, 0)
+    sends = []
+    for j in (2, 3, 1):
+        p = lax.rem(q + j, 4)
+        sends.append(remote(so.at[p], ro.at[q], ss3.at[j, 0], rs3.at[j, 0], plane0 + p))
+        sends.append(remote(sl.at[p], rl.at[q], ss3.at[j, 1], rs3.at[j, 1], plane0 + p))
+    for send in sends:
+        send.start()
+    oacc[...] = jnp.zeros_like(oacc)
+    loads[4].wait()
+    for j in (1, 2, 3):
+        p = lax.rem(q + 4 - j, 4)
+        remote(so.at[p], ro.at[p], ss3.at[j, 0], rs3.at[j, 0], plane0 + p).wait_recv()
+        remote(sl.at[p], rl.at[p], ss3.at[j, 1], rs3.at[j, 1], plane0 + p).wait_recv()
+    froms = [lax.rem(q + j, 4) for j in (1, 2, 3)]
+    for h in range(2):
+        lses = [sl[q, h : h + 1, :]] + [rl[p, h : h + 1, :] for p in froms]
+        rows = slice(h * HEAD_DIM, (h + 1) * HEAD_DIM)
+        parts = [so[q, rows, :]] + [ro[p, rows, :] for p in froms]
+        top = jnp.maximum(jnp.maximum(lses[0], lses[1]), jnp.maximum(lses[2], lses[3]))
+        shares = [jnp.exp(lse - top) for lse in lses]
+        whole = shares[0] + shares[1] + shares[2] + shares[3]
+        mixed = sum(part.astype(jnp.float32) * share for part, share in zip(parts, shares)) / whole
+        at[me, :, rows] = jnp.transpose(mixed).astype(jnp.bfloat16)
+
+    def project_out(i, slots):
+        width = slots.shape[2]
+        first = pl.multiple_of(i * width, width)
+        oacc[...] += jnp.dot(slots[i], wo[pl.ds(first, width), :], preferred_element_type=jnp.float32)
+
+    finish_second = gather(at, at.at[me], ss4, rs4, project_out, lambda k: None)
+    out_ref[...] = oacc[...].astype(jnp.bfloat16)
+    finish_first()
+    finish_second()
+    for k in range(1, 4):
+        kv_copy(k).wait_send()
+    pcp(q, 0, yn).wait_send()
+    pcp(q, 1, sib).wait_send()
+    pcp(yq, 1, sib).wait_send()
+    for send in sends:
+        send.wait_send()
+
+
+KV_AFTER = 1
+
+
+def fused_body(
+    hidden_in, norm_gain, w_query, w_key, w_value, w_out, cache_keys, cache_values, offset, length
+):
+    tokens, depth = hidden_in.shape
+    keys = cache_keys.shape[0]
+    hidden = jnp.concatenate([hidden_in, jnp.broadcast_to(norm_gain, (PAD_ROWS, depth))], axis=0)
+    kv = jnp.transpose(jnp.stack([cache_keys, cache_values]), (2, 0, 1, 3))
+    half_dim = HEAD_DIM // 2
+    inverse = ROPE_BASE ** (-(jnp.arange(half_dim, dtype=jnp.float32) * 2.0 / HEAD_DIM))
+    positions = offset[0] + jnp.arange(tokens, dtype=jnp.int32)
+    angles = positions.astype(jnp.float32)[:, None] * inverse[None, :]
+    cosine, sine = jnp.cos(angles), jnp.sin(angles)
+    cosine = jnp.concatenate([cosine, cosine], axis=1)
+    sine = jnp.concatenate([-sine, sine], axis=1)
+    smem = pl.BlockSpec(memory_space=pltpu.SMEM)
+    vmem = pl.BlockSpec(memory_space=pltpu.VMEM)
+    hbm = pl.BlockSpec(memory_space=pl.ANY)
+    bf16, f32 = jnp.bfloat16, jnp.float32
+    dma = pltpu.SemaphoreType.DMA
+    n = FUSED_DEVICES
+    return pl.pallas_call(
+        fused_kernel,
+        out_shape=jax.ShapeDtypeStruct((tokens, w_out.shape[1]), bf16),
+        in_specs=[smem, smem, hbm, hbm, hbm, hbm, hbm, hbm, vmem, vmem],
+        out_specs=vmem,
+        scratch_shapes=[
+            pltpu.VMEM((n, tokens + PAD_ROWS, depth), bf16),
+            pltpu.VMEM(w_query.shape, bf16),
+            pltpu.VMEM((64, w_query.shape[0]), bf16),
+            pltpu.VMEM(w_out.shape, bf16),
+            pltpu.VMEM((PLANES, 2, keys, HEAD_DIM), bf16),
+            pltpu.VMEM((PLANE, tokens, 384), bf16),
+            pltpu.VMEM((8, HEAD_DIM, tokens), f32),
+            pltpu.VMEM((8, 1, tokens), f32),
+            pltpu.VMEM((8, 1, tokens), f32),
+            pltpu.VMEM((PLANE, 2 * HEAD_DIM, tokens), bf16),
+            pltpu.VMEM((PLANE, 8, tokens), f32),
+            pltpu.VMEM((PLANE, 2 * HEAD_DIM, tokens), bf16),
+            pltpu.VMEM((PLANE, 8, tokens), f32),
+            pltpu.VMEM((n, tokens, 2 * HEAD_DIM), bf16),
+            pltpu.VMEM((tokens, 128), f32),
+            pltpu.VMEM((tokens, 2 * HEAD_DIM), f32),
+            pltpu.VMEM((tokens, 64), f32),
+            pltpu.VMEM((tokens, w_out.shape[1]), f32),
+            dma((n, 4)), dma((n,)),
+            dma((PLANES,)), dma((PLANES,)),
+            dma((PLANE, 2)), dma((PLANE,)),
+            dma((4, 2)), dma((4, 2)),
+            dma((n, 4)), dma((n,)),
+            dma((6,)),
+        ],
+        compiler_params=pltpu.CompilerParams(
+            collective_id=0, has_side_effects=True, vmem_limit_bytes=50 * 1024 * 1024
+        ),
+        cost_estimate=pl.CostEstimate(flops=6_000_000_000, bytes_accessed=16_000_000, transcendentals=6_000_000),
+    )(offset, length, hidden, w_query, w_key.T, w_value.T, w_out, kv, cosine, sine)
+
+
 def solution(mesh):
+    body = fused_body if mesh.shape["weight"] == FUSED_DEVICES else general_body
     return jax.shard_map(
         body,
         mesh=mesh,

time: 345 us -> 117 us (0.34)
  blocking collectives: 143 us -> 0 us
  Pallas kernels: 0 us -> 112 us
  waiting for transfers between devices: 107 us -> 0 us
  matrix products: 34.5 us -> 0 us
  other arithmetic: 24.8 us -> 0.87 us
  local copies, waits for them, and re-layouts: 16.7 us -> 2.81 us
  between operations: 15.2 us -> 1.48 us
  starting transfers between devices: 3.79 us -> 0 us
    pallas_call x0 -> x1, Pallas kernels: none -> 112 us  [fused_body(): pl.pallas_call(fused_kernel, out_shape=jax.ShapeDtypeStruct((tokens, w_ou...]
    all_gather x3 -> x0, waiting for transfers between devices: 88.4 us -> none  [the longest x1 40.6 us: body(): attention = lax.all_gather(attention_share, 'weight', axis=1, tiled=True)]
    pmax x1 -> x0, blocking collectives: 60 us -> none  [body(): lax.pmax(local_peak.astype(jnp.bfloat16), 'weight').astype(local_peak.dtype)]
    psum x1 -> x0, blocking collectives: 58.9 us -> none  [body(): denominator = lax.psum(local_total * factor, 'weight')]
    dot_general x21 -> x0, matrix products: 34.5 us -> none  [the longest x4 8.71 us: body(): jnp.einsum('tgd,kd->tgk', grouped, cache_keys[:, group, :], preferred_ele...]
    all_gather x1 -> x0, blocking collectives: 23.7 us -> none  [body(): lax.all_gather(norm_gain, 'weight', axis=1, tiled=True)]
    reduce_sum x6 -> x0, other arithmetic: 12.6 us -> none  [the longest x5 9.33 us: body(): total = jnp.sum(prefix_weights, axis=-1) + jnp.sum(fresh_weights, axis=-1)]
    reduce_scatter x1 -> x0, waiting for transfers between devices: 11.1 us -> none  [body(): lax.psum_scatter(scaled_mixed, 'weight', scatter_dimension=1, tiled=True)]
  transfers between devices with their start and end apart: 5 -> 0, of which waited for: 5 -> 0; matrix products, arithmetic and copies ran while one was open for 4% -> 0% of each run, Pallas kernels for 0% -> 0%
where the time goes in v1:
time: 117 us
  Pallas kernels  112 us (96%)
  local copies, waits for them, and re-layouts  2.81 us (2%)
  between operations  1.48 us (1%)
    pallas_call x1, Pallas kernels, fused_body(): pl.pallas_call(fused_kernel, out_shape=jax.ShapeDtypeStruct((tokens, w_ou...  112 us

profile of v1, /device:TPU:0, one launch (start us, length us, event | category | flops | bytes accessed | tf_op | source)
XLA Modules:
  0.0 116.9 jit_solution(3133012292243600979)
XLA Ops:
  0.0 0.0 copy-start.2
  0.8 0.5 fusion
  1.3 0.1 pad_maximum_fusion.1
  1.4 0.0 copy-done.2
  1.4 1.3 %copy_bitcast_fusion = (bf16[1,768,4,128]{3,1,0,2:T(8,128)(2,1)S(1)}, bf16[1,768,4,128]{3,1,0,2:T(8,128)(2,1)S(1)}) fusion(bf16[768,4,128]{2,1,0:T(4,128)(2,1)S(1)} %copy-done.2, bf16[768,4,128]{2,1,0:T(4,128)(2,1)} %param.16), kind=kLoop, calls=%fused_computation.1 | loop fusion | bytes 3145728 | tf_op jit(solution)/shard_map/stack | solution.py:441
  2.8 0.0 copy-start.4
  2.8 0.0 copy-start.3
  2.8 0.0 copy-start
  2.8 0.0 copy-start.1
  2.8 0.1 maximum_bitcast_fusion.kv
  3.0 0.5 copy-done.4
  3.5 0.3 copy-done.3
  4.4 0.0 copy-done
  4.4 0.0 copy-done.1
  4.5 111.8 %shard_map.100 = bf16[256,512]{1,0:T(8,128)(2,1)S(1)} custom-call(s32[1]{0:T(128)} %copy.16.start_ref, s32[1]{0:T(128)S(6)} %copy.17.length_ref, bf16[272,512]{1,0:T(8,128)(2,1)S(1)} %pad_maximum_fusion.hidden, bf16[8192,256]{1,0:T(8,128)(2,1)} %w_query.1, bf16[32,8192]{1,0:T(8,128)(2,1)S(1)} %bitcast.10, bf16[32,8192]{1,0:T(8,128)(2,1)S(1)} %bitcast.11, ...), custom_call_target="tpu_custom_call" | custom-call | flops 6000000000 | bytes 16000000 | tf_op jit(solution)/shard_map/pallas_call | solution.py:455
  116.2 0.7 copy.18
  (5 shorter events, 0.1 us)
Async XLA Ops:
  0.0 1.4 %copy-start.2 = (bf16[768,4,128]{2,1,0:T(4,128)(2,1)S(1)}, bf16[768,4,128]{2,1,0:T(4,128)(2,1)}, u32[]{:S(2)}) copy-start(bf16[768,4,128]{2,1,0:T(4,128)(2,1)} %param.17) | copy-start | bytes 2359300
  2.8 0.7 copy-start.4
  2.8 1.0 copy-start.3
  2.8 1.6 %copy-start = (bf16[8192,32]{0,1:T(8,128)(2,1)S(1)}, bf16[8192,32]{0,1:T(8,128)(2,1)}, u32[]{:S(2)}) copy-start(bf16[8192,32]{0,1:T(8,128)(2,1)} %param.13) | copy-start | bytes 1572868
  2.8 1.6 %copy-start.1 = (bf16[8192,32]{0,1:T(8,128)(2,1)S(1)}, bf16[8192,32]{0,1:T(8,128)(2,1)}, u32[]{:S(2)}) copy-start(bf16[8192,32]{0,1:T(8,128)(2,1)} %param.14) | copy-start | bytes 1572868

commit v2 on v0

--- a/solution.py
+++ b/solution.py
@@ -1,8 +1,11 @@
+import functools
 import math
 
 import jax
 import jax.numpy as jnp
 from jax import lax
+from jax.experimental import pallas as pl
+from jax.experimental.pallas import tpu as pltpu
 from jax.sharding import PartitionSpec as P
 
 QHEADS = 32
@@ -28,7 +31,7 @@
     )
 
 
-def body(
+def general_body(
     hidden_in, norm_gain, w_query, w_key, w_value, w_out, cache_keys, cache_values, offset, length
 ):
     my_index = lax.axis_index("weight")
@@ -125,7 +128,421 @@
     return jnp.dot(attention, w_out, preferred_element_type=jnp.float32).astype(jnp.bfloat16)
 
 
+PLANES = 4
+PLANE = 4
+PAD_ROWS = 16
+FUSED_DEVICES = PLANES * PLANE
+
+
+def near_order(z):
+    half = lax.div(z, 2)
+    return [z, z + 1 - 2 * lax.rem(z, 2), 2 - half, 3 * (1 - half)]
+
+
+def fused_kernel(
+    start_ref, length_ref, hidden, w_query, wk_t, wv_t, w_out, kv, cos_ref, sin_ref,
+    out_ref,
+    xg, wq, wkv, wo, kb, vb, vt, pq, acc, peak, total, so, sl, ro, rl, at, rinv, qacc, kacc, oacc,
+    ss1, rs1, sskv, rskv, ss2, rs2, ss3, rs3, ss4, rs4, local_sem,
+):
+    me = lax.axis_index("weight")
+    z = lax.div(me, 4)
+    y = lax.rem(lax.div(me, 2), 2)
+    c = lax.rem(me, 2)
+    q = lax.rem(me, 4)
+    plane0 = z * 4
+    up, down = me + 4, me - 4
+    yn = me + 2 - 4 * y
+    sib = me + 1 - 2 * c
+    ynsib = yn + 1 - 2 * c
+    order = near_order(z)
+    tokens = out_ref.shape[0]
+    depth = xg.shape[2]
+    keys = kb.shape[1]
+
+    def remote(src, dst, ssem, rsem, dev):
+        return pltpu.make_async_remote_copy(
+            src_ref=src, dst_ref=dst, send_sem=ssem, recv_sem=rsem,
+            device_id={"weight": dev}, device_id_type=pl.DeviceIdType.MESH,
+        )
+
+    barrier = pltpu.get_barrier_semaphore()
+    for k in range(1, 4):
+        for dev in (order[k] * 4 + q, plane0 + lax.rem(q + k, 4)):
+            pl.semaphore_signal(
+                barrier, inc=1, device_id={"weight": dev}, device_id_type=pl.DeviceIdType.MESH
+            )
+    pl.semaphore_wait(barrier, 6)
+
+    def gather(slots, own, ss, rs, direct):
+        def cp(i, src, d, dev):
+            return remote(src, slots.at[i], ss.at[i, d], rs.at[i], dev)
+
+        def along(i, src, first, act):
+            if direct:
+                if first:
+                    for k in range(1, 4):
+                        act(cp(i, src, 3 + k, order[k] * 4 + q))
+                return
+            o = lax.div(i, 4)
+
+            @pl.when((o <= z) & (z < 3))
+            def _():
+                act(cp(i, src, 0, up))
+
+            @pl.when((o >= z) & (z > 0))
+            def _():
+                act(cp(i, src, 1, down))
+
+        def across(i, src, act):
+            act(cp(i, src, 2, yn))
+            act(cp(i, src, 3, sib))
+
+        def begin():
+            along(me, own, True, lambda copy: copy.start())
+            across(me, own, lambda copy: copy.start())
+
+        def forward(k):
+            if k < 3:
+                i = order[k + 1] * 4 + q
+                cp(i, slots.at[i], 2, yn).wait_recv()
+                along(i, slots.at[i], False, lambda copy: copy.start())
+                across(i, slots.at[i], lambda copy: copy.start())
+            i = order[k] * 4 + lax.rem(yn, 4)
+            cp(i, slots.at[i], 2, yn).wait_recv()
+            cp(i, slots.at[i], 3, sib).start()
+
+        def consume(k, use):
+            use(order[k] * 4 + q)
+            use(order[k] * 4 + lax.rem(yn, 4))
+            for other in (sib, ynsib):
+                i = order[k] * 4 + lax.rem(other, 4)
+                cp(i, slots.at[i], 3, sib).wait_recv()
+                use(i)
+
+        def finish():
+            along(me, own, True, lambda copy: copy.wait_send())
+            across(me, own, lambda copy: copy.wait_send())
+            for k in range(1, 4):
+                i = order[k] * 4 + q
+                along(i, slots.at[i], False, lambda copy: copy.wait_send())
+                across(i, slots.at[i], lambda copy: copy.wait_send())
+            for k in range(4):
+                i = order[k] * 4 + lax.rem(yn, 4)
+                cp(i, slots.at[i], 3, sib).wait_send()
+
+        return begin, forward, consume, finish
+
+    own_copy = pltpu.make_async_copy(hidden, xg.at[me], local_sem.at[0])
+    loads = [
+        pltpu.make_async_copy(w_query, wq, local_sem.at[1]),
+        pltpu.make_async_copy(wk_t, wkv.at[pl.ds(0, 32)], local_sem.at[2]),
+        pltpu.make_async_copy(wv_t, wkv.at[pl.ds(32, 32)], local_sem.at[3]),
+        pltpu.make_async_copy(kv.at[z, 0], kb.at[z], local_sem.at[4]),
+        pltpu.make_async_copy(kv.at[z, 1], vb.at[z], local_sem.at[6]),
+        pltpu.make_async_copy(w_out, wo, local_sem.at[5]),
+    ]
+
+    def kv_copies(k):
+        o = order[k]
+        return [
+            remote(kv.at[o, j], buf.at[z], sskv.at[o, j], rskv.at[z, j], o * 4 + q)
+            for j, buf in enumerate((kb, vb))
+        ]
+
+    def kv_arrivals(k):
+        o = order[k]
+        return [
+            remote(kv.at[o, j], buf.at[o], sskv.at[o, j], rskv.at[o, j], o * 4 + q)
+            for j, buf in enumerate((kb, vb))
+        ]
+
+    def between_first(k):
+        if k == -1:
+            own_copy.start()
+            for load in loads:
+                load.start()
+            rinv[...] = jnp.zeros_like(rinv)
+            own_copy.wait()
+        if k == KV_AFTER:
+            for j in range(1, 4):
+                for copy in kv_copies(j):
+                    copy.start()
+
+    def squares(i):
+        x = xg[i, 0:tokens, :].astype(jnp.float32)
+        xx = x * x
+        part = xx[:, 0:128]
+        for j in range(1, depth // 128):
+            part = part + xx[:, j * 128 : (j + 1) * 128]
+        rinv[...] += part
+
+    begin, forward, consume, finish_first = gather(xg, hidden, ss1, rs1, False)
+    begin()
+    between_first(-1)
+    for k in range(4):
+        forward(k)
+        between_first(k)
+        consume(k, squares)
+
+    mean = jnp.sum(rinv[...], axis=1, keepdims=True) * (1.0 / (depth * FUSED_DEVICES))
+    rinv[...] = jnp.broadcast_to(lax.rsqrt(mean + EPSILON), rinv.shape)
+    for load in loads[:3]:
+        load.wait()
+    qacc[...] = jnp.zeros_like(qacc)
+    kacc[...] = jnp.zeros_like(kacc)
+
+    def project(i, carry):
+        x = xg[i, 0:tokens, :].astype(jnp.float32)
+        gain = xg[i, tokens : tokens + 1, :].astype(jnp.float32)
+        scale = jnp.concatenate([rinv[...]] * (depth // 128), axis=1)
+        normed = (x * scale * gain).astype(jnp.bfloat16)
+        first = pl.multiple_of(i * depth, depth)
+        qacc[...] += jnp.dot(normed, wq[pl.ds(first, depth), :], preferred_element_type=jnp.float32)
+        kacc[...] += lax.dot_general(
+            wkv[:, pl.ds(first, depth)], normed, (((1,), (1,)), ((), ())),
+            preferred_element_type=jnp.float32,
+        )
+        return carry
+
+    lax.fori_loop(0, FUSED_DEVICES, project, 0)
+
+    def turn(x):
+        return x * cos_ref[...] + pltpu.roll(x, 64, 1) * sin_ref[...]
+
+    queries = qacc[...].astype(jnp.bfloat16).astype(jnp.float32)
+    for h in range(2):
+        rows = slice(h * HEAD_DIM, (h + 1) * HEAD_DIM)
+        pq[q, rows, :] = jnp.transpose(turn(queries[:, rows])).astype(jnp.bfloat16)
+    pq[q, 256:320, :] = kacc[...].astype(jnp.bfloat16)
+
+    def pcp(i, d, dev):
+        return remote(pq.at[i], pq.at[i], ss2.at[i, d], rs2.at[i], dev)
+
+    yq, sq, ysq = lax.rem(yn, 4), lax.rem(sib, 4), lax.rem(ynsib, 4)
+    near = [q, yq, ysq, sq]
+    pcp(q, 0, yn).start()
+    pcp(q, 1, sib).start()
+
+    loads[3].wait()
+    loads[4].wait()
+    for k in range(1, 4):
+        for copy in kv_arrivals(k):
+            copy.wait_recv()
+    for o in range(PLANES):
+        vt[:, o * keys : (o + 1) * keys] = jnp.transpose(vb[o])
+
+    start = start_ref[0]
+    length = length_ref[0]
+    score_scale = math.log2(math.e) / math.sqrt(HEAD_DIM)
+
+    def attend(query, blocks):
+        top = whole = mixed = None
+        for key_rows, value_cols, allowed in blocks:
+            scores = jnp.dot(key_rows, query, preferred_element_type=jnp.float32) * score_scale
+            if allowed is not None:
+                scores = jnp.where(allowed, scores, NEG_FILL)
+            new = jnp.max(scores, axis=0, keepdims=True)
+            if top is not None:
+                new = jnp.maximum(top, new)
+            weights = jnp.exp2(scores - new)
+            part = jnp.sum(weights, axis=0, keepdims=True)
+            product = jnp.dot(
+                value_cols, weights.astype(jnp.bfloat16), preferred_element_type=jnp.float32
+            )
+            if top is not None:
+                factor = jnp.exp2(top - new)
+                part = part + whole * factor
+                product = product + mixed * factor
+            top, whole, mixed = new, part, product
+        return top, whole, mixed
+
+    def cache_blocks():
+        row = lax.broadcasted_iota(jnp.int32, (keys, tokens), 0)
+        last = row < start - ((PLANES - 1) * 4 + q) * keys
+        return [
+            (kb[o], vt[:, o * keys : (o + 1) * keys], last if o == PLANES - 1 else None)
+            for o in range(PLANES)
+        ]
+
+    def head_rows(h):
+        if isinstance(h, int):
+            return pl.ds(h * HEAD_DIM, HEAD_DIM)
+        return pl.ds(pl.multiple_of(h * HEAD_DIM, HEAD_DIM), HEAD_DIM)
+
+    def keep(n, result):
+        top, whole, mixed = result
+        so[n] = (mixed * (1.0 / whole)).astype(jnp.bfloat16)
+        sl[n, 0:1, :] = top + jnp.log2(whole)
+        sl[n, 1:8, :] = jnp.zeros((7, tokens), jnp.float32)
+
+    def mine(h, carry):
+        peak[h], total[h], acc[h] = attend(pq[q, head_rows(h), :], cache_blocks())
+        return carry
+
+    lax.fori_loop(0, 2, mine, 0)
+
+    pcp(yq, 0, yn).wait_recv()
+    pcp(yq, 1, sib).start()
+    pcp(sq, 1, sib).wait_recv()
+
+    def part_copies(t, h, p, back):
+        n = p * 2 + h
+        m = q * 2 + h
+        target = n if back else m
+        return [
+            remote(so.at[n], ro.at[target], ss3.at[t, h, 0], rs3.at[t, h, 0], plane0 + p),
+            remote(sl.at[n], rl.at[target], ss3.at[t, h, 1], rs3.at[t, h, 1], plane0 + p),
+        ]
+
+    def theirs(t, h):
+        p = near[t]
+        keep(p * 2 + h, attend(pq[p, head_rows(h), :], cache_blocks()))
+        for copy in part_copies(t, h, p, False):
+            copy.start()
+
+    theirs(1, 0)
+    pcp(ysq, 1, sib).wait_recv()
+    fresh_key = jnp.transpose(
+        jnp.concatenate([pq[p, 256:288, :] for p in range(PLANE)], axis=0).astype(jnp.float32)
+    )
+    fresh_key = turn(fresh_key).astype(jnp.bfloat16)
+    fresh_value = jnp.concatenate([pq[p, 288:320, :] for p in range(PLANE)], axis=0)
+    row = lax.broadcasted_iota(jnp.int32, (tokens, tokens), 0)
+    token = lax.broadcasted_iota(jnp.int32, (tokens, tokens), 1)
+    fresh_ok = (row <= token) & (row < length - start)
+    for h in range(2):
+        top, whole, mixed = attend(
+            pq[q, head_rows(h), :], [(fresh_key, fresh_value, fresh_ok)]
+        )
+        new = jnp.maximum(top, peak[h])
+        one, two = jnp.exp2(top - new), jnp.exp2(peak[h] - new)
+        keep(q * 2 + h, (new, whole * one + total[h] * two, mixed * one + acc[h] * two))
+    theirs(2, 0)
+    theirs(3, 0)
+
+    gathers = [gather(at.at[h], at.at[h, me], ss4.at[h], rs4.at[h], True) for h in range(2)]
+
+    def combine(h):
+        for t in range(1, 4):
+            for copy in part_copies(t, h, near[t], True):
+                copy.wait_recv()
+        lses = [sl[q * 2 + h, 0:1, :]] + [rl[near[t] * 2 + h, 0:1, :] for t in range(1, 4)]
+        parts = [so[q * 2 + h]] + [ro[near[t] * 2 + h] for t in range(1, 4)]
+        top = jnp.maximum(jnp.maximum(lses[0], lses[1]), jnp.maximum(lses[2], lses[3]))
+        shares = [jnp.exp2(lse - top) for lse in lses]
+        whole = shares[0] + shares[1] + shares[2] + shares[3]
+        mixed = sum(part.astype(jnp.float32) * share for part, share in zip(parts, shares)) / whole
+        at[h, me] = jnp.transpose(mixed).astype(jnp.bfloat16)
+        gathers[h][0]()
+
+    def project_out(h):
+        def use(i):
+            first = pl.multiple_of((i * 2 + h) * HEAD_DIM, HEAD_DIM)
+            oacc[...] += jnp.dot(
+                at[h, i], wo[pl.ds(first, HEAD_DIM), :], preferred_element_type=jnp.float32
+            )
+        return use
+
+    oacc[...] = jnp.zeros_like(oacc)
+    loads[5].wait()
+    theirs(1, 1)
+    combine(0)
+    theirs(2, 1)
+    gathers[0][1](0)
+    theirs(3, 1)
+    gathers[0][1](1)
+    combine(1)
+    gathers[0][1](2)
+    gathers[0][1](3)
+    gathers[1][1](0)
+    for k in range(4):
+        gathers[0][2](k, project_out(0))
+        if k < 3:
+            gathers[1][1](k + 1)
+    for k in range(4):
+        gathers[1][2](k, project_out(1))
+    out_ref[...] = oacc[...].astype(jnp.bfloat16)
+    finish_first()
+    for h in range(2):
+        gathers[h][3]()
+    for k in range(1, 4):
+        for copy in kv_copies(k):
+            copy.wait_send()
+    pcp(q, 0, yn).wait_send()
+    pcp(q, 1, sib).wait_send()
+    pcp(yq, 1, sib).wait_send()
+    for t in range(1, 4):
+        for h in range(2):
+            for copy in part_copies(t, h, near[t], False):
+                copy.wait_send()
+
+
+KV_AFTER = 1
+
+
+def fused_body(
+    hidden_in, norm_gain, w_query, w_key, w_value, w_out, cache_keys, cache_values, offset, length
+):
+    tokens, depth = hidden_in.shape
+    keys = cache_keys.shape[0]
+    hidden = jnp.concatenate([hidden_in, jnp.broadcast_to(norm_gain, (PAD_ROWS, depth))], axis=0)
+    kv = jnp.transpose(jnp.stack([cache_keys, cache_values]), (2, 0, 1, 3))
+    half_dim = HEAD_DIM // 2
+    inverse = ROPE_BASE ** (-(jnp.arange(half_dim, dtype=jnp.float32) * 2.0 / HEAD_DIM))
+    positions = offset[0] + jnp.arange(tokens, dtype=jnp.int32)
+    angles = positions.astype(jnp.float32)[:, None] * inverse[None, :]
+    cosine, sine = jnp.cos(angles), jnp.sin(angles)
+    cosine = jnp.concatenate([cosine, cosine], axis=1)
+    sine = jnp.concatenate([-sine, sine], axis=1)
+    smem = pl.BlockSpec(memory_space=pltpu.SMEM)
+    vmem = pl.BlockSpec(memory_space=pltpu.VMEM)
+    hbm = pl.BlockSpec(memory_space=pl.ANY)
+    bf16, f32 = jnp.bfloat16, jnp.float32
+    dma = pltpu.SemaphoreType.DMA
+    n = FUSED_DEVICES
+    return pl.pallas_call(
+        fused_kernel,
+        out_shape=jax.ShapeDtypeStruct((tokens, w_out.shape[1]), bf16),
+        in_specs=[smem, smem, hbm, hbm, hbm, hbm, hbm, hbm, vmem, vmem],
+        out_specs=vmem,
+        scratch_shapes=[
+            pltpu.VMEM((n, tokens + PAD_ROWS, depth), bf16),
+            pltpu.VMEM(w_query.shape, bf16),
+            pltpu.VMEM((64, w_query.shape[0]), bf16),
+            pltpu.VMEM(w_out.shape, bf16),
+            pltpu.VMEM((PLANES, keys, HEAD_DIM), bf16),
+            pltpu.VMEM((PLANES, keys, HEAD_DIM), bf16),
+            pltpu.VMEM((HEAD_DIM, PLANES * keys), bf16),
+            pltpu.VMEM((PLANE, 320, tokens), bf16),
+            pltpu.VMEM((2, HEAD_DIM, tokens), f32),
+            pltpu.VMEM((2, 1, tokens), f32),
+            pltpu.VMEM((2, 1, tokens), f32),
+            pltpu.VMEM((8, HEAD_DIM, tokens), bf16),
+            pltpu.VMEM((8, 8, tokens), f32),
+            pltpu.VMEM((8, HEAD_DIM, tokens), bf16),
+            pltpu.VMEM((8, 8, tokens), f32),
+            pltpu.VMEM((2, n, tokens, HEAD_DIM), bf16),
+            pltpu.VMEM((tokens, 128), f32),
+            pltpu.VMEM((tokens, 2 * HEAD_DIM), f32),
+            pltpu.VMEM((64, tokens), f32),
+            pltpu.VMEM((tokens, w_out.shape[1]), f32),
+            dma((n, 4)), dma((n,)),
+            dma((PLANES, 2)), dma((PLANES, 2)),
+            dma((PLANE, 2)), dma((PLANE,)),
+            dma((4, 2, 2)), dma((4, 2, 2)),
+            dma((2, n, 7)), dma((2, n)),
+            dma((7,)),
+        ],
+        compiler_params=pltpu.CompilerParams(
+            collective_id=0, has_side_effects=True, vmem_limit_bytes=50 * 1024 * 1024
+        ),
+        cost_estimate=pl.CostEstimate(flops=6_000_000_000, bytes_accessed=16_000_000, transcendentals=6_000_000),
+    )(offset, length, hidden, w_query, w_key.T, w_value.T, w_out, kv, cosine, sine)
+
+
 def solution(mesh):
+    body = fused_body if mesh.shape["weight"] == FUSED_DEVICES else general_body
     return jax.shard_map(
         body,
         mesh=mesh,

time: 345 us -> 101 us (0.29)
  blocking collectives: 143 us -> 0 us
  waiting for transfers between devices: 107 us -> 0 us
  Pallas kernels: 0 us -> 95.4 us
  matrix products: 34.5 us -> 0 us
  other arithmetic: 24.8 us -> 0.87 us
  local copies, waits for them, and re-layouts: 16.7 us -> 2.81 us
  between operations: 15.2 us -> 1.48 us
  starting transfers between devices: 3.79 us -> 0 us
    pallas_call x0 -> x1, Pallas kernels: none -> 95.4 us  [fused_body(): pl.pallas_call(fused_kernel, out_shape=jax.ShapeDtypeStruct((tokens, w_ou...]
    all_gather x3 -> x0, waiting for transfers between devices: 88.4 us -> none  [the longest x1 40.6 us: body(): attention = lax.all_gather(attention_share, 'weight', axis=1, tiled=True)]
    pmax x1 -> x0, blocking collectives: 60 us -> none  [body(): lax.pmax(local_peak.astype(jnp.bfloat16), 'weight').astype(local_peak.dtype)]
    psum x1 -> x0, blocking collectives: 58.9 us -> none  [body(): denominator = lax.psum(local_total * factor, 'weight')]
    dot_general x21 -> x0, matrix products: 34.5 us -> none  [the longest x4 8.71 us: body(): jnp.einsum('tgd,kd->tgk', grouped, cache_keys[:, group, :], preferred_ele...]
    all_gather x1 -> x0, blocking collectives: 23.7 us -> none  [body(): lax.all_gather(norm_gain, 'weight', axis=1, tiled=True)]
    reduce_sum x6 -> x0, other arithmetic: 12.6 us -> none  [the longest x5 9.33 us: body(): total = jnp.sum(prefix_weights, axis=-1) + jnp.sum(fresh_weights, axis=-1)]
    reduce_scatter x1 -> x0, waiting for transfers between devices: 11.1 us -> none  [body(): lax.psum_scatter(scaled_mixed, 'weight', scatter_dimension=1, tiled=True)]
  transfers between devices with their start and end apart: 5 -> 0, of which waited for: 5 -> 0; matrix products, arithmetic and copies ran while one was open for 4% -> 0% of each run, Pallas kernels for 0% -> 0%
where the time goes in v2:
time: 101 us
  Pallas kernels  95.4 us (94%)
  local copies, waits for them, and re-layouts  2.81 us (3%)
  between operations  1.48 us (1%)
    pallas_call x1, Pallas kernels, fused_body(): pl.pallas_call(fused_kernel, out_shape=jax.ShapeDtypeStruct((tokens, w_ou...  95.4 us

profile of v2, /device:TPU:0, one launch (start us, length us, event | category | flops | bytes accessed | tf_op | source)
XLA Modules:
  0.0 100.6 jit_solution(13640607842494662809)
XLA Ops:
  0.0 0.0 copy-start.2
  0.8 0.5 fusion
  1.3 0.1 pad_maximum_fusion.1
  1.4 0.0 copy-done.2
  1.4 1.3 %copy_bitcast_fusion = (bf16[1,768,4,128]{3,1,0,2:T(8,128)(2,1)S(1)}, bf16[1,768,4,128]{3,1,0,2:T(8,128)(2,1)S(1)}) fusion(bf16[768,4,128]{2,1,0:T(4,128)(2,1)S(1)} %copy-done.2, bf16[768,4,128]{2,1,0:T(4,128)(2,1)} %param.16), kind=kLoop, calls=%fused_computation.1 | loop fusion | bytes 3145728 | tf_op jit(solution)/shard_map/stack | solution.py:490
  2.8 0.0 copy-start.4
  2.8 0.0 copy-start.3
  2.8 0.0 copy-start
  2.8 0.0 copy-start.1
  2.8 0.1 maximum_bitcast_fusion.kv
  3.0 0.5 copy-done.4
  3.5 0.3 copy-done.3
  4.4 0.0 copy-done
  4.4 0.0 copy-done.1
  4.5 95.4 %shard_map.100 = bf16[256,512]{1,0:T(8,128)(2,1)S(1)} custom-call(s32[1]{0:T(128)} %copy.16.start_ref, s32[1]{0:T(128)S(6)} %copy.17.length_ref, bf16[272,512]{1,0:T(8,128)(2,1)S(1)} %pad_maximum_fusion.hidden, bf16[8192,256]{1,0:T(8,128)(2,1)} %w_query.1, bf16[32,8192]{1,0:T(8,128)(2,1)S(1)} %bitcast.10, bf16[32,8192]{1,0:T(8,128)(2,1)S(1)} %bitcast.11, ...), custom_call_target="tpu_custom_call" | custom-call | flops 6000000000 | bytes 16000000 | tf_op jit(solution)/shard_map/pallas_call | solution.py:504
  99.9 0.7 copy.18
  (5 shorter events, 0.1 us)
Async XLA Ops:
  0.0 1.4 %copy-start.2 = (bf16[768,4,128]{2,1,0:T(4,128)(2,1)S(1)}, bf16[768,4,128]{2,1,0:T(4,128)(2,1)}, u32[]{:S(2)}) copy-start(bf16[768,4,128]{2,1,0:T(4,128)(2,1)} %param.17) | copy-start | bytes 2359300
  2.8 0.7 copy-start.4
  2.8 1.0 copy-start.3
  2.8 1.6 %copy-start = (bf16[8192,32]{0,1:T(8,128)(2,1)S(1)}, bf16[8192,32]{0,1:T(8,128)(2,1)}, u32[]{:S(2)}) copy-start(bf16[8192,32]{0,1:T(8,128)(2,1)} %param.13) | copy-start | bytes 1572868
  2.8 1.6 %copy-start.1 = (bf16[8192,32]{0,1:T(8,128)(2,1)S(1)}, bf16[8192,32]{0,1:T(8,128)(2,1)}, u32[]{:S(2)}) copy-start(bf16[8192,32]{0,1:T(8,128)(2,1)} %param.14) | copy-start | bytes 1572868

commit v3 on v2

--- a/solution.py
+++ b/solution.py
@@ -140,10 +140,10 @@
 
 
 def fused_kernel(
-    start_ref, length_ref, hidden, w_query, wk_t, wv_t, w_out, kv, cos_ref, sin_ref,
+    start_ref, length_ref, hidden, w_query, wk_t, wv_t, w_out, kv, cos_hbm, sin_hbm,
     out_ref,
-    xg, wq, wkv, wo, kb, vb, vt, pq, acc, peak, total, so, sl, ro, rl, at, rinv, qacc, kacc, oacc,
-    ss1, rs1, sskv, rskv, ss2, rs2, ss3, rs3, ss4, rs4, local_sem,
+    cos_ref, sin_ref, stats, xg, wq, wkv, wo, kb, vb, vt, pq, acc, peak, total, so, sl, ro, rl, at, rinv, qacc, kacc, oacc,
+    ssst, rsst, ss1, rs1, sskv, rskv, ss2, rs2, ss3, rs3, ss4, rs4, local_sem,
 ):
     me = lax.axis_index("weight")
     z = lax.div(me, 4)
@@ -157,7 +157,8 @@
     ynsib = yn + 1 - 2 * c
     order = near_order(z)
     tokens = out_ref.shape[0]
-    depth = xg.shape[2]
+    half = tokens // 2
+    depth = xg.shape[3]
     keys = kb.shape[1]
 
     def remote(src, dst, ssem, rsem, dev):
@@ -167,12 +168,29 @@
         )
 
     barrier = pltpu.get_barrier_semaphore()
-    for k in range(1, 4):
-        for dev in (order[k] * 4 + q, plane0 + lax.rem(q + k, 4)):
-            pl.semaphore_signal(
-                barrier, inc=1, device_id={"weight": dev}, device_id_type=pl.DeviceIdType.MESH
-            )
-    pl.semaphore_wait(barrier, 6)
+    for j in range(1, FUSED_DEVICES):
+        pl.semaphore_signal(
+            barrier, inc=1, device_id={"weight": lax.rem(me + j, FUSED_DEVICES)},
+            device_id_type=pl.DeviceIdType.MESH,
+        )
+    own_copy = pltpu.make_async_copy(hidden, xg.at[me], local_sem.at[0])
+    own_copy.start()
+    own_copy.wait()
+    for side in range(2):
+        x = xg[me, side, 0:half, :].astype(jnp.float32)
+        xx = x * x
+        part = xx[:, 0:128]
+        for j in range(1, depth // 128):
+            part = part + xx[:, j * 128 : (j + 1) * 128]
+        row_sum = jnp.sum(jnp.transpose(part), axis=0, keepdims=True)
+        stats[me, :, side * half : (side + 1) * half] = jnp.broadcast_to(row_sum, (8, half))
+    pl.semaphore_wait(barrier, FUSED_DEVICES - 1)
+
+    def stat_copy(j, slot, dev):
+        return remote(stats.at[slot], stats.at[slot], ssst.at[j], rsst.at[j], dev)
+
+    for j in range(1, FUSED_DEVICES):
+        stat_copy(j, me, lax.rem(me + j, FUSED_DEVICES)).start()
 
     def gather(slots, own, ss, rs, direct):
         def cp(i, src, d, dev):
@@ -212,13 +230,17 @@
             cp(i, slots.at[i], 2, yn).wait_recv()
             cp(i, slots.at[i], 3, sib).start()
 
+        def last(k):
+            for other in (sib, ynsib):
+                i = order[k] * 4 + lax.rem(other, 4)
+                cp(i, slots.at[i], 3, sib).wait_recv()
+
         def consume(k, use):
             use(order[k] * 4 + q)
             use(order[k] * 4 + lax.rem(yn, 4))
-            for other in (sib, ynsib):
-                i = order[k] * 4 + lax.rem(other, 4)
-                cp(i, slots.at[i], 3, sib).wait_recv()
-                use(i)
+            last(k)
+            use(order[k] * 4 + lax.rem(sib, 4))
+            use(order[k] * 4 + lax.rem(ynsib, 4))
 
         def finish():
             along(me, own, True, lambda copy: copy.wait_send())
@@ -231,9 +253,8 @@
                 i = order[k] * 4 + lax.rem(yn, 4)
                 cp(i, slots.at[i], 3, sib).wait_send()
 
-        return begin, forward, consume, finish
-
-    own_copy = pltpu.make_async_copy(hidden, xg.at[me], local_sem.at[0])
+        return begin, forward, consume, finish, last
+
     loads = [
         pltpu.make_async_copy(w_query, wq, local_sem.at[1]),
         pltpu.make_async_copy(wk_t, wkv.at[pl.ds(0, 32)], local_sem.at[2]),
@@ -241,6 +262,8 @@
         pltpu.make_async_copy(kv.at[z, 0], kb.at[z], local_sem.at[4]),
         pltpu.make_async_copy(kv.at[z, 1], vb.at[z], local_sem.at[6]),
         pltpu.make_async_copy(w_out, wo, local_sem.at[5]),
+        pltpu.make_async_copy(cos_hbm, cos_ref, local_sem.at[7]),
+        pltpu.make_async_copy(sin_hbm, sin_ref, local_sem.at[8]),
     ]
 
     def kv_copies(k):
@@ -257,44 +280,20 @@
             for j, buf in enumerate((kb, vb))
         ]
 
-    def between_first(k):
-        if k == -1:
-            own_copy.start()
-            for load in loads:
-                load.start()
-            rinv[...] = jnp.zeros_like(rinv)
-            own_copy.wait()
-        if k == KV_AFTER:
-            for j in range(1, 4):
-                for copy in kv_copies(j):
-                    copy.start()
-
-    def squares(i):
-        x = xg[i, 0:tokens, :].astype(jnp.float32)
-        xx = x * x
-        part = xx[:, 0:128]
-        for j in range(1, depth // 128):
-            part = part + xx[:, j * 128 : (j + 1) * 128]
-        rinv[...] += part
-
-    begin, forward, consume, finish_first = gather(xg, hidden, ss1, rs1, False)
-    begin()
-    between_first(-1)
-    for k in range(4):
-        forward(k)
-        between_first(k)
-        consume(k, squares)
-
-    mean = jnp.sum(rinv[...], axis=1, keepdims=True) * (1.0 / (depth * FUSED_DEVICES))
-    rinv[...] = jnp.broadcast_to(lax.rsqrt(mean + EPSILON), rinv.shape)
-    for load in loads[:3]:
-        load.wait()
+    firsts = [
+        gather(xg.at[:, side], hidden.at[side], ss1.at[side], rs1.at[side], False)
+        for side in range(2)
+    ]
+    for first in firsts:
+        first[0]()
+    for load in loads:
+        load.start()
     qacc[...] = jnp.zeros_like(qacc)
     kacc[...] = jnp.zeros_like(kacc)
 
-    def project(i, carry):
-        x = xg[i, 0:tokens, :].astype(jnp.float32)
-        gain = xg[i, tokens : tokens + 1, :].astype(jnp.float32)
+    def project(i):
+        x = jnp.concatenate([xg[i, side, 0:half, :] for side in range(2)], axis=0).astype(jnp.float32)
+        gain = xg[i, 0, half : half + 1, :].astype(jnp.float32)
         scale = jnp.concatenate([rinv[...]] * (depth // 128), axis=1)
         normed = (x * scale * gain).astype(jnp.bfloat16)
         first = pl.multiple_of(i * depth, depth)
@@ -303,9 +302,44 @@
             wkv[:, pl.ds(first, depth)], normed, (((1,), (1,)), ((), ())),
             preferred_element_type=jnp.float32,
         )
-        return carry
-
-    lax.fori_loop(0, FUSED_DEVICES, project, 0)
+
+    def pair(k, one, two):
+        def step(j, carry):
+            project(order[k] * 4 + one + j * (two - one))
+            return carry
+
+        lax.fori_loop(0, 2, step, 0)
+
+    def project_last(k):
+        for first in firsts:
+            first[4](k)
+        pair(k, lax.rem(sib, 4), lax.rem(ynsib, 4))
+
+    for k in range(4):
+        for first in firsts:
+            first[1](k)
+        if k == KV_AFTER:
+            for j in range(1, 4):
+                for copy in kv_copies(j):
+                    copy.start()
+        if k == 0:
+            for j in range(1, FUSED_DEVICES):
+                sender = lax.rem(me + FUSED_DEVICES - j, FUSED_DEVICES)
+                stat_copy(j, sender, sender).wait_recv()
+            sums = stats[0]
+            for i in range(1, FUSED_DEVICES):
+                sums = sums + stats[i]
+            scale_row = lax.rsqrt(sums[0:1] * (1.0 / (depth * FUSED_DEVICES)) + EPSILON)
+            rinv[...] = jnp.transpose(jnp.broadcast_to(scale_row, (128, tokens)))
+            for load in loads[:3]:
+                load.wait()
+        pair(k, q, lax.rem(yn, 4))
+        if k > 0:
+            project_last(k - 1)
+    project_last(3)
+
+    loads[6].wait()
+    loads[7].wait()
 
     def turn(x):
         return x * cos_ref[...] + pltpu.roll(x, 64, 1) * sin_ref[...]
@@ -326,18 +360,11 @@
 
     loads[3].wait()
     loads[4].wait()
-    for k in range(1, 4):
-        for copy in kv_arrivals(k):
-            copy.wait_recv()
-    for o in range(PLANES):
-        vt[:, o * keys : (o + 1) * keys] = jnp.transpose(vb[o])
-
     start = start_ref[0]
     length = length_ref[0]
     score_scale = math.log2(math.e) / math.sqrt(HEAD_DIM)
 
-    def attend(query, blocks):
-        top = whole = mixed = None
+    def attend(query, blocks, top=None, whole=None, mixed=None):
         for key_rows, value_cols, allowed in blocks:
             scores = jnp.dot(key_rows, query, preferred_element_type=jnp.float32) * score_scale
             if allowed is not None:
@@ -361,7 +388,7 @@
         row = lax.broadcasted_iota(jnp.int32, (keys, tokens), 0)
         last = row < start - ((PLANES - 1) * 4 + q) * keys
         return [
-            (kb[o], vt[:, o * keys : (o + 1) * keys], last if o == PLANES - 1 else None)
+            (kb[o], vt[o], last if o == PLANES - 1 else None)
             for o in range(PLANES)
         ]
 
@@ -376,14 +403,30 @@
         sl[n, 0:1, :] = top + jnp.log2(whole)
         sl[n, 1:8, :] = jnp.zeros((7, tokens), jnp.float32)
 
-    def mine(h, carry):
-        peak[h], total[h], acc[h] = attend(pq[q, head_rows(h), :], cache_blocks())
-        return carry
-
-    lax.fori_loop(0, 2, mine, 0)
-
-    pcp(yq, 0, yn).wait_recv()
-    pcp(yq, 1, sib).start()
+    def mine(k, o):
+        row = lax.broadcasted_iota(jnp.int32, (keys, tokens), 0)
+        allowed = row < start - (o * 4 + q) * keys
+
+        def one(h, carry):
+            before = () if k == 0 else (peak[h], total[h], acc[h])
+            peak[h], total[h], acc[h] = attend(
+                pq[q, head_rows(h), :], [(kb[o], vt[o], allowed)], *before
+            )
+            return carry
+
+        lax.fori_loop(0, 2, one, 0)
+
+    for k in range(4):
+        o = order[k]
+        if k > 0:
+            for copy in kv_arrivals(k):
+                copy.wait_recv()
+        vt[o] = jnp.transpose(vb[o])
+        if k == 3:
+            pcp(yq, 0, yn).wait_recv()
+            pcp(yq, 1, sib).start()
+        mine(k, o)
+
     pcp(sq, 1, sib).wait_recv()
 
     def part_copies(t, h, p, back):
@@ -463,7 +506,10 @@
     for k in range(4):
         gathers[1][2](k, project_out(1))
     out_ref[...] = oacc[...].astype(jnp.bfloat16)
-    finish_first()
+    for first in firsts:
+        first[3]()
+    for j in range(1, FUSED_DEVICES):
+        stat_copy(j, me, lax.rem(me + j, FUSED_DEVICES)).wait_send()
     for h in range(2):
         gathers[h][3]()
     for k in range(1, 4):
@@ -486,7 +532,8 @@
 ):
     tokens, depth = hidden_in.shape
     keys = cache_keys.shape[0]
-    hidden = jnp.concatenate([hidden_in, jnp.broadcast_to(norm_gain, (PAD_ROWS, depth))], axis=0)
+    halves = hidden_in.reshape(2, tokens // 2, depth)
+    hidden = jnp.concatenate([halves, jnp.broadcast_to(norm_gain, (2, PAD_ROWS, depth))], axis=1)
     kv = jnp.transpose(jnp.stack([cache_keys, cache_values]), (2, 0, 1, 3))
     half_dim = HEAD_DIM // 2
     inverse = ROPE_BASE ** (-(jnp.arange(half_dim, dtype=jnp.float32) * 2.0 / HEAD_DIM))
@@ -504,16 +551,19 @@
     return pl.pallas_call(
         fused_kernel,
         out_shape=jax.ShapeDtypeStruct((tokens, w_out.shape[1]), bf16),
-        in_specs=[smem, smem, hbm, hbm, hbm, hbm, hbm, hbm, vmem, vmem],
+        in_specs=[smem, smem, hbm, hbm, hbm, hbm, hbm, hbm, hbm, hbm],
         out_specs=vmem,
         scratch_shapes=[
-            pltpu.VMEM((n, tokens + PAD_ROWS, depth), bf16),
+            pltpu.VMEM((tokens, HEAD_DIM), f32),
+            pltpu.VMEM((tokens, HEAD_DIM), f32),
+            pltpu.VMEM((n, 8, tokens), f32),
+            pltpu.VMEM((n, 2, tokens // 2 + PAD_ROWS, depth), bf16),
             pltpu.VMEM(w_query.shape, bf16),
             pltpu.VMEM((64, w_query.shape[0]), bf16),
             pltpu.VMEM(w_out.shape, bf16),
             pltpu.VMEM((PLANES, keys, HEAD_DIM), bf16),
             pltpu.VMEM((PLANES, keys, HEAD_DIM), bf16),
-            pltpu.VMEM((HEAD_DIM, PLANES * keys), bf16),
+            pltpu.VMEM((PLANES, HEAD_DIM, keys), bf16),
             pltpu.VMEM((PLANE, 320, tokens), bf16),
             pltpu.VMEM((2, HEAD_DIM, tokens), f32),
             pltpu.VMEM((2, 1, tokens), f32),
@@ -527,12 +577,13 @@
             pltpu.VMEM((tokens, 2 * HEAD_DIM), f32),
             pltpu.VMEM((64, tokens), f32),
             pltpu.VMEM((tokens, w_out.shape[1]), f32),
-            dma((n, 4)), dma((n,)),
+            dma((n,)), dma((n,)),
+            dma((2, n, 4)), dma((2, n)),
             dma((PLANES, 2)), dma((PLANES, 2)),
             dma((PLANE, 2)), dma((PLANE,)),
             dma((4, 2, 2)), dma((4, 2, 2)),
             dma((2, n, 7)), dma((2, n)),
-            dma((7,)),
+            dma((9,)),
         ],
         compiler_params=pltpu.CompilerParams(
             collective_id=0, has_side_effects=True, vmem_limit_bytes=50 * 1024 * 1024

time: 101 us -> 102 us (level)
  Pallas kernels: 95.4 us -> 96.7 us
    pallas_call x1, Pallas kernels: 95.4 us -> 96.7 us  [fused_body(): pl.pallas_call(fused_kernel, out_shape=jax.ShapeDtypeStruct((tokens, w_ou...]
where the time goes in v3:
time: 102 us
  Pallas kernels  96.7 us (95%)
  local copies, waits for them, and re-layouts  2.81 us (3%)
  between operations  1.48 us (1%)
    pallas_call x1, Pallas kernels, fused_body(): pl.pallas_call(fused_kernel, out_shape=jax.ShapeDtypeStruct((tokens, w_ou...  96.7 us

profile of v3, /device:TPU:0, one launch (start us, length us, event | category | flops | bytes accessed | tf_op | source)
XLA Modules:
  0.0 101.9 jit_solution(6138603779974125097)
XLA Ops:
  0.0 0.0 copy-start.2
  0.8 0.5 fusion
  1.3 0.1 pad_maximum_fusion.1
  1.4 0.0 copy-done.2
  1.4 1.3 %copy_bitcast_fusion = (bf16[1,768,4,128]{3,1,0,2:T(8,128)(2,1)S(1)}, bf16[1,768,4,128]{3,1,0,2:T(8,128)(2,1)S(1)}) fusion(bf16[768,4,128]{2,1,0:T(4,128)(2,1)S(1)} %copy-done.2, bf16[768,4,128]{2,1,0:T(4,128)(2,1)} %param.16), kind=kLoop, calls=%fused_computation.1 | loop fusion | bytes 3145728 | tf_op jit(solution)/shard_map/stack | solution.py:537
  2.8 0.0 copy-start.4
  2.8 0.0 copy-start.3
  2.8 0.0 copy-start
  2.8 0.0 copy-start.1
  2.8 0.1 maximum_bitcast_fusion.kv
  3.0 0.5 copy-done.4
  3.5 0.3 copy-done.3
  4.4 0.0 copy-done
  4.4 0.0 copy-done.1
  4.5 96.7 %shard_map.103 = bf16[256,512]{1,0:T(8,128)(2,1)S(1)} custom-call(s32[1]{0:T(128)} %copy.16.start_ref, s32[1]{0:T(128)S(6)} %copy.17.length_ref, bf16[2,144,512]{2,1,0:T(8,128)(2,1)S(1)} %pad_maximum_fusion.hidden, bf16[8192,256]{1,0:T(8,128)(2,1)} %w_query.1, bf16[32,8192]{1,0:T(8,128)(2,1)S(1)} %bitcast.11, bf16[32,8192]{1,0:T(8,128)(2,1)S(1)} %bitcast.12, ...), custom_call_target="tpu_custom_call" | custom-call | flops 6000000000 | bytes 16000000 | tf_op jit(solution)/shard_map/pallas_call | solution.py:551
  101.2 0.7 copy.18
  (5 shorter events, 0.1 us)
Async XLA Ops:
  0.0 1.4 %copy-start.2 = (bf16[768,4,128]{2,1,0:T(4,128)(2,1)S(1)}, bf16[768,4,128]{2,1,0:T(4,128)(2,1)}, u32[]{:S(2)}) copy-start(bf16[768,4,128]{2,1,0:T(4,128)(2,1)} %param.17) | copy-start | bytes 2359300
  2.8 0.7 copy-start.4
  2.8 1.0 copy-start.3
  2.8 1.6 %copy-start = (bf16[8192,32]{0,1:T(8,128)(2,1)S(1)}, bf16[8192,32]{0,1:T(8,128)(2,1)}, u32[]{:S(2)}) copy-start(bf16[8192,32]{0,1:T(8,128)(2,1)} %param.13) | copy-start | bytes 1572868
  2.8 1.6 %copy-start.1 = (bf16[8192,32]{0,1:T(8,128)(2,1)S(1)}, bf16[8192,32]{0,1:T(8,128)(2,1)}, u32[]{:S(2)}) copy-start(bf16[8192,32]{0,1:T(8,128)(2,1)} %param.14) | copy-start | bytes 1572868
